TPU v7x, 32 devices: a whole 2x2x4 slice. The times are simulated.
32 devices in a mesh: dp: 4 (over y, x), cp: 8 (over z, core).
Axes of the slice: x: 2, y: 2, z: 4, core: 2. Of those that a mesh axis runs over, the one named last changes fastest.
Arguments:
- tokens: bfloat16 [4096, 1536], P(('dp', 'cp')), may hold values from -6 to 6
- output_cotangent: bfloat16 [4096, 1536], P(('dp', 'cp')), may hold values from -6 to 6
- sequence_lengths: int32 [4, 4], P('dp'), may hold values from 1 to 512, as said below
- block_order: int32 [4, 8], P('dp'), may hold values from 0 to 7, as said below
- attn_input: float32 [1536, 2560], P(('dp', 'cp')), may hold values from -0.15625 to 0.15625
- input_moment: float32 [1536, 2560], P(('dp', 'cp')), may hold values from -40 to 40
- input_square: float32 [1536, 2560], P(('dp', 'cp')), may hold values from 217.088 to 860.16
- attn_output: float32 [1536, 1536], P(('dp', 'cp')), may hold values from -1.25 to 1.25
- output_moment: float32 [1536, 1536], P(('dp', 'cp')), may hold values from -5 to 5
- output_square: float32 [1536, 1536], P(('dp', 'cp')), may hold values from 3.36 to 13.6
- gate_up: float32 [1536, 13824], P(('dp', 'cp')), may hold values from -0.15625 to 0.15625
- gateup_moment: float32 [1536, 13824], P(('dp', 'cp')), may hold values from -8 to 8
- gateup_square: float32 [1536, 13824], P(('dp', 'cp')), may hold values from 8.6016 to 34.4064
- down_weight: float32 [6912, 1536], P(('dp', 'cp')), may hold values from -0.078125 to 0.078125
- down_moment: float32 [6912, 1536], P(('dp', 'cp')), may hold values from -20 to 20
- down_square: float32 [6912, 1536], P(('dp', 'cp')), may hold values from 53.248 to 217.088
- norm_gains: float32 [3200], replicated, may hold values from 0.5 to 1.5
- gains_moment: float32 [3200], replicated, may hold values from -40 to 40
- gains_square: float32 [3200], replicated, may hold values from 217.088 to 860.16
Outputs:
- mixed: bfloat16 [4096, 1536], P(('dp', 'cp'))
- token_gradient: float32 [4096, 1536], P(('dp', 'cp'))
- input_next: float32 [1536, 2560], P(('dp', 'cp'))
- input_moment_next: float32 [1536, 2560], P(('dp', 'cp'))
- input_square_next: float32 [1536, 2560], P(('dp', 'cp'))
- output_next: float32 [1536, 1536], P(('dp', 'cp'))
- output_moment_next: float32 [1536, 1536], P(('dp', 'cp'))
- output_square_next: float32 [1536, 1536], P(('dp', 'cp'))
- gateup_next: float32 [1536, 13824], P(('dp', 'cp'))
- gateup_moment_next: float32 [1536, 13824], P(('dp', 'cp'))
- gateup_square_next: float32 [1536, 13824], P(('dp', 'cp'))
- down_next: float32 [6912, 1536], P(('dp', 'cp'))
- down_moment_next: float32 [6912, 1536], P(('dp', 'cp'))
- down_square_next: float32 [6912, 1536], P(('dp', 'cp'))
- gains_next: float32 [3200], replicated
- gains_moment_next: float32 [3200], replicated
- gains_square_next: float32 [3200], replicated
Inputs may be any that keep to these rules, and one draw needn't show every extreme that they name: `sequence_lengths`: each row holds 4 lengths, packed in order into its group's 1024 positions and summing to 1024; the largest in each row is exactly 512. `block_order`: each row is a permutation of the 8 blocks of its group's packed tokens.
All inputs are finite; a program needn't handle non-finite values.
Results may differ from a plain program's by a relative error of at most 0.025.
Values may be sent and summed in bfloat16 or wider, within the bound.
A program may use at most 384 MiB of HBM per device.

v0:
```python
import math

import jax
import jax.numpy as jnp
from jax import lax
from jax.sharding import PartitionSpec as P

HEADS = 24
KV_HEADS = 8
HEAD_DIM = 64
FF = 6912
STEP = 10


norm_eps = 1e-05
rope_base = 1000000.0
beta_one = 0.9
beta_two = 0.95
adam_eps = 1e-08
rate_input = 0.06
rate_output = 0.9
rate_gateup = 0.06
rate_down = 0.03
rate_gains = 0.5
weight_decay = 0.1
masked_score = -1e30


def rope_tables(offsets):
    half_dim = HEAD_DIM // 2
    freqs = jnp.exp(
        jnp.arange(half_dim, dtype=jnp.float32) * (-2.0 * math.log(rope_base) / HEAD_DIM)
    )
    angles = offsets.astype(jnp.float32)[:, None] * freqs[None, :]
    return (jnp.cos(angles), jnp.sin(angles))


def rotate(values, cosine, sine):
    half_dim = HEAD_DIM // 2
    first_half = values[..., :half_dim]
    second_half = values[..., half_dim:]
    cos_wide = cosine[:, None, :]
    sin_wide = sine[:, None, :]
    return jnp.concatenate(
        [
            first_half * cos_wide - second_half * sin_wide,
            second_half * cos_wide + first_half * sin_wide,
        ],
        axis=-1,
    )


def locate(positions, lengths):
    seq_ends = jnp.cumsum(lengths)
    starts = seq_ends - lengths
    doc_index = jnp.sum((positions[:, None] >= seq_ends[None, :]).astype(jnp.int32), axis=1)
    picked = (doc_index[:, None] == jnp.arange(lengths.shape[0], dtype=jnp.int32)[None, :]).astype(
        jnp.int32
    )
    return (doc_index, positions - jnp.sum(picked * starts[None, :], axis=1))


def rms_parts(values):
    inverse = lax.rsqrt(jnp.mean(values * values, axis=-1, keepdims=True) + norm_eps)
    return (values * inverse, inverse)


def norm_back(d_normed, normal_hat, inverse):
    return inverse * (
        d_normed - normal_hat * jnp.mean(d_normed * normal_hat, axis=-1, keepdims=True)
    )


def contract_rows(left, right):
    return lax.dot_general(
        left, right, (((0,), (0,)), ((), ())), preferred_element_type=jnp.float32
    )


def contract_cols(left, right):
    return lax.dot_general(
        left, right, (((1,), (1,)), ((), ())), preferred_element_type=jnp.float32
    )


def owner_order(values, data_count, context_count):
    lead = values.shape[0]
    each = values.shape[1] // (data_count * context_count)
    return (
        values.reshape(lead, data_count, context_count, each)
        .transpose(0, 2, 1, 3)
        .reshape(lead, values.shape[1])
    )


def adam_update(weight, first_moment, second_moment, gradient, rate, decay):
    first_moment = beta_one * first_moment + (1.0 - beta_one) * gradient
    second_moment = beta_two * second_moment + (1.0 - beta_two) * gradient * gradient
    first_fix = 1.0 - beta_one**STEP
    second_fix = 1.0 - beta_two**STEP
    direction = first_moment / first_fix / (jnp.sqrt(second_moment / second_fix) + adam_eps)
    return (weight - rate * (direction + decay * weight), first_moment, second_moment)


def on_device(
    tokens,
    output_cotangent,
    sequence_lengths,
    block_order,
    attn_input,
    input_moment,
    input_square,
    attn_output,
    output_moment,
    output_square,
    gate_up,
    gateup_moment,
    gateup_square,
    down_weight,
    down_moment,
    down_square,
    norm_gains,
    gains_moment,
    gains_square,
):
    row_count = tokens.shape[0]
    model_width = tokens.shape[1]
    q_width = HEADS * HEAD_DIM
    kv_width = KV_HEADS * HEAD_DIM
    proj_width = q_width + 2 * kv_width
    head_groups = HEADS // KV_HEADS
    score_scale = HEAD_DIM ** (-0.5)
    gain_one = norm_gains[:model_width]
    gain_two = norm_gains[model_width : 2 * model_width]
    gain_query = norm_gains[2 * model_width : 2 * model_width + HEAD_DIM]
    gain_key = norm_gains[2 * model_width + HEAD_DIM :]
    seq_lens = sequence_lengths[0]
    order_row = block_order[0]
    context_count = lax.axis_size("cp")
    data_count = lax.axis_size("dp")
    own_slot = lax.axis_index("cp")
    offsets = jnp.arange(row_count, dtype=jnp.int32)
    own_block = jnp.sum(
        jnp.where(jnp.arange(context_count, dtype=jnp.int32) == own_slot, order_row, 0)
    )
    positions = own_block * row_count + offsets
    key_positions = (order_row[:, None] * row_count + offsets[None, :]).reshape(
        context_count * row_count
    )
    doc_index, seq_offset = locate(positions, seq_lens)
    key_doc = locate(key_positions, seq_lens)[0]
    cosine, sine = rope_tables(seq_offset)
    input_bf = attn_input.astype(jnp.bfloat16)
    output_bf = attn_output.astype(jnp.bfloat16)
    gateup_bf = gate_up.astype(jnp.bfloat16)
    down_bf = down_weight.astype(jnp.bfloat16)
    input_all, output_all = (
        lax.all_gather(input_bf, ("dp", "cp"), axis=0, tiled=True),
        lax.all_gather(output_bf, ("dp", "cp"), axis=0, tiled=True),
    )
    x_float = tokens.astype(jnp.float32)
    hat_one, inv_one = rms_parts(x_float)
    normed_one = (hat_one * gain_one).astype(jnp.bfloat16)
    projected = jnp.dot(normed_one, input_all, preferred_element_type=jnp.float32)
    query_raw = projected[:, :q_width].reshape(row_count, HEADS, HEAD_DIM)
    key_raw = projected[:, q_width : q_width + kv_width].reshape(row_count, KV_HEADS, HEAD_DIM)
    value_raw = projected[:, q_width + kv_width :]
    hat_query, inv_query = rms_parts(query_raw)
    hat_key, inv_key = rms_parts(key_raw)
    queries = rotate(hat_query * gain_query, cosine, sine).astype(jnp.bfloat16)
    key_rot = rotate(hat_key * gain_key, cosine, sine)
    key_value = jnp.concatenate([key_rot.reshape(row_count, kv_width), value_raw], axis=1).astype(
        jnp.bfloat16
    )
    kv_all = lax.all_gather(key_value, "cp", axis=0, tiled=True)
    total_keys = kv_all.shape[0]
    key_span = min(512, total_keys)
    block_count = total_keys // key_span
    kv_blocks = kv_all.reshape(block_count, key_span, 2 * kv_width)
    pos_blocks = key_positions.reshape(block_count, key_span)
    doc_blocks = key_doc.reshape(block_count, key_span)
    query_group = queries.reshape(row_count, KV_HEADS, head_groups, HEAD_DIM)

    def block_scores(kv_block, key_pos, key_docs):
        key_block = kv_block[:, :kv_width].reshape(key_span, KV_HEADS, HEAD_DIM)
        value_block = kv_block[:, kv_width:].reshape(key_span, KV_HEADS, HEAD_DIM)
        scores = (
            jnp.einsum("qhgd,khd->hgqk", query_group, key_block, preferred_element_type=jnp.float32)
            * score_scale
        )
        allowed = (doc_index[:, None] == key_docs[None, :]) & (
            key_pos[None, :] <= positions[:, None]
        )
        return (key_block, value_block, jnp.where(allowed, scores, masked_score), allowed)

    def forward_block(carry, items):
        run_max, run_total, run_sum = carry
        key_block, value_block, scores, allowed = block_scores(*items)
        new_max = jnp.maximum(run_max, jnp.max(scores, axis=-1))
        weights = jnp.where(allowed, jnp.exp(scores - new_max[..., None]), 0.0)
        factor = jnp.exp(run_max - new_max)
        run_total = run_total * factor + jnp.sum(weights, axis=-1)
        run_sum = run_sum * factor[..., None] + jnp.einsum(
            "hgqk,khd->hgqd",
            weights.astype(jnp.bfloat16),
            value_block,
            preferred_element_type=jnp.float32,
        )
        return ((new_max, run_total, run_sum), None)

    start_state = (
        jnp.full((KV_HEADS, head_groups, row_count), masked_score, jnp.float32),
        jnp.zeros((KV_HEADS, head_groups, row_count), jnp.float32),
        jnp.zeros((KV_HEADS, head_groups, row_count, HEAD_DIM), jnp.float32),
    )
    (run_max, run_total, run_sum), unused = lax.scan(
        forward_block, start_state, (kv_blocks, pos_blocks, doc_blocks)
    )
    attended = run_sum / run_total[..., None]
    log_total = run_max + jnp.log(run_total)
    attn_flat = attended.transpose(2, 0, 1, 3).reshape(row_count, q_width).astype(jnp.bfloat16)
    residual = x_float + jnp.dot(attn_flat, output_all, preferred_element_type=jnp.float32)
    hat_two, inv_two = rms_parts(residual)
    normed_two = (hat_two * gain_two).astype(jnp.bfloat16)
    columns = normed_two
    gate_both = jnp.dot(
        columns,
        lax.all_gather(gateup_bf, ("dp", "cp"), axis=0, tiled=True),
        preferred_element_type=jnp.float32,
    )
    gate_part = gate_both[:, :FF]
    up_part = gate_both[:, FF:]
    gate_sig = jax.nn.sigmoid(gate_part)
    gate_act = gate_part * gate_sig
    hidden = (gate_act * up_part).astype(jnp.bfloat16)
    columns = hidden
    ff_result = jnp.dot(
        columns,
        lax.all_gather(down_bf, ("dp", "cp"), axis=0, tiled=True),
        preferred_element_type=jnp.float32,
    )
    mixed = (residual + ff_result).astype(jnp.bfloat16)
    d_hidden = contract_cols(
        output_cotangent, lax.all_gather(down_bf, ("dp", "cp"), axis=0, tiled=True)
    )
    d_gate = d_hidden * up_part * (gate_sig * (1.0 + gate_part * (1.0 - gate_sig)))
    d_up = d_hidden * gate_act
    d_gate_both = jnp.concatenate([d_gate, d_up], axis=1).astype(jnp.bfloat16)
    d_normed_two = contract_cols(
        d_gate_both, lax.all_gather(gateup_bf, ("dp", "cp"), axis=0, tiled=True)
    )
    grad_gain_two = jnp.sum(d_normed_two * hat_two, axis=0)
    d_residual = output_cotangent.astype(jnp.float32) + norm_back(
        d_normed_two * gain_two, hat_two, inv_two
    )
    d_branch = d_residual.astype(jnp.bfloat16)
    input_back, output_back = (input_all, output_all)
    d_flat = contract_cols(d_branch, output_back).astype(jnp.bfloat16)
    d_attended = d_flat.reshape(row_count, KV_HEADS, head_groups, HEAD_DIM).transpose(1, 2, 0, 3)
    delta = jnp.sum(d_attended.astype(jnp.float32) * attended, axis=-1)

    def backward_block(d_query_sum, items):
        key_block, value_block, scores, allowed = block_scores(*items)
        probs = jnp.where(allowed, jnp.exp(scores - log_total[..., None]), 0.0)
        d_probs = jnp.einsum(
            "hgqd,khd->hgqk", d_attended, value_block, preferred_element_type=jnp.float32
        )
        d_scores = (probs * (d_probs - delta[..., None])).astype(jnp.bfloat16)
        d_query_sum = (
            d_query_sum
            + jnp.einsum("hgqk,khd->hgqd", d_scores, key_block, preferred_element_type=jnp.float32)
            * score_scale
        )
        d_keys = (
            jnp.einsum("hgqk,qhgd->khd", d_scores, query_group, preferred_element_type=jnp.float32)
            * score_scale
        )
        d_values = jnp.einsum(
            "hgqk,hgqd->khd",
            probs.astype(jnp.bfloat16),
            d_attended,
            preferred_element_type=jnp.float32,
        )
        return (
            d_query_sum,
            jnp.concatenate(
                [d_keys.reshape(key_span, kv_width), d_values.reshape(key_span, kv_width)], axis=1
            ),
        )

    d_query_sum, d_kv_blocks = lax.scan(
        backward_block,
        jnp.zeros((KV_HEADS, head_groups, row_count, HEAD_DIM), jnp.float32),
        (kv_blocks, pos_blocks, doc_blocks),
    )
    d_kv = lax.psum_scatter(
        d_kv_blocks.reshape(total_keys, 2 * kv_width).astype(jnp.bfloat16),
        "cp",
        scatter_dimension=0,
        tiled=True,
    ).astype(jnp.float32)
    d_query_rot = rotate(
        d_query_sum.transpose(2, 0, 1, 3).reshape(row_count, HEADS, HEAD_DIM), cosine, -sine
    )
    grad_gain_query = jnp.sum(d_query_rot * hat_query, axis=(0, 1))
    d_query_raw = norm_back(d_query_rot * gain_query, hat_query, inv_query)
    d_key_rot = rotate(d_kv[:, :kv_width].reshape(row_count, KV_HEADS, HEAD_DIM), cosine, -sine)
    grad_gain_key = jnp.sum(d_key_rot * hat_key, axis=(0, 1))
    d_key_raw = norm_back(d_key_rot * gain_key, hat_key, inv_key)
    d_projected = jnp.concatenate(
        [
            d_query_raw.reshape(row_count, q_width),
            d_key_raw.reshape(row_count, kv_width),
            d_kv[:, kv_width:],
        ],
        axis=1,
    ).astype(jnp.bfloat16)
    d_normed_one = contract_cols(d_projected, input_back)
    grad_gain_one = jnp.sum(d_normed_one * hat_one, axis=0)
    token_gradient = d_residual + norm_back(d_normed_one * gain_one, hat_one, inv_one)

    def make_wide(first_src, attn_src, second_src):

        def wide_terms(row_start, row_total):
            return jnp.concatenate(
                [
                    contract_rows(first_src, d_projected),
                    contract_rows(attn_src, d_branch),
                    contract_rows(second_src, d_gate_both),
                ],
                axis=1,
            )

        return wide_terms

    def make_down(hidden_src):

        def down_terms(row_start, row_total):
            return contract_rows(hidden_src, output_cotangent)

        return down_terms

    shard_rows = attn_input.shape[0]
    down_rows = down_weight.shape[0]
    wide_fn = make_wide(
        owner_order(normed_one, data_count, context_count),
        owner_order(attn_flat, data_count, context_count),
        owner_order(normed_two, data_count, context_count),
    )
    down_fn = make_down(owner_order(hidden, data_count, context_count))
    group_wide = lax.psum_scatter(
        wide_fn(jnp.int32(0), lax.axis_size("cp") * (shard_rows * data_count)).astype(jnp.bfloat16),
        "cp",
        scatter_dimension=0,
        tiled=True,
    )
    group_down = lax.psum_scatter(
        down_fn(jnp.int32(0), lax.axis_size("cp") * (down_rows * data_count)).astype(jnp.bfloat16),
        "cp",
        scatter_dimension=0,
        tiled=True,
    )
    wide_grads, down_grads = (
        lax.psum_scatter(group_wide, "dp", scatter_dimension=0, tiled=True).astype(jnp.float32),
        lax.psum_scatter(group_down, "dp", scatter_dimension=0, tiled=True).astype(jnp.float32),
    )
    gain_grads = lax.psum(
        jnp.concatenate([grad_gain_one, grad_gain_two, grad_gain_query, grad_gain_key]),
        ("dp", "cp"),
    )
    grad_input = wide_grads[:, :proj_width]
    grad_output = wide_grads[:, proj_width : proj_width + model_width]
    grad_gateup = wide_grads[:, proj_width + model_width :]
    input_next, input_moment_next, input_square_next = adam_update(
        attn_input, input_moment, input_square, grad_input, rate_input, weight_decay
    )
    output_next, output_moment_next, output_square_next = adam_update(
        attn_output, output_moment, output_square, grad_output, rate_output, weight_decay
    )
    gateup_next, gateup_moment_next, gateup_square_next = adam_update(
        gate_up, gateup_moment, gateup_square, grad_gateup, rate_gateup, weight_decay
    )
    down_next, down_moment_next, down_square_next = adam_update(
        down_weight, down_moment, down_square, down_grads, rate_down, weight_decay
    )
    gains_next, gains_moment_next, gains_square_next = adam_update(
        norm_gains, gains_moment, gains_square, gain_grads, rate_gains, 0.0
    )
    return (
        mixed,
        token_gradient,
        input_next,
        input_moment_next,
        input_square_next,
        output_next,
        output_moment_next,
        output_square_next,
        gateup_next,
        gateup_moment_next,
        gateup_square_next,
        down_next,
        down_moment_next,
        down_square_next,
        gains_next,
        gains_moment_next,
        gains_square_next,
    )


def solution(mesh):
    in_specs = (
        P(("dp", "cp"), None),
        P(("dp", "cp"), None),
        P("dp", None),
        P("dp", None),
        P(("dp", "cp"), None),
        P(("dp", "cp"), None),
        P(("dp", "cp"), None),
        P(("dp", "cp"), None),
        P(("dp", "cp"), None),
        P(("dp", "cp"), None),
        P(("dp", "cp"), None),
        P(("dp", "cp"), None),
        P(("dp", "cp"), None),
        P(("dp", "cp"), None),
        P(("dp", "cp"), None),
        P(("dp", "cp"), None),
        P(),
        P(),
        P(),
    )
    out_specs = (
        P(("dp", "cp"), None),
        P(("dp", "cp"), None),
        P(("dp", "cp"), None),
        P(("dp", "cp"), None),
        P(("dp", "cp"), None),
        P(("dp", "cp"), None),
        P(("dp", "cp"), None),
        P(("dp", "cp"), None),
        P(("dp", "cp"), None),
        P(("dp", "cp"), None),
        P(("dp", "cp"), None),
        P(("dp", "cp"), None),
        P(("dp", "cp"), None),
        P(("dp", "cp"), None),
        P(),
        P(),
        P(),
    )
    return jax.shard_map(
        on_device, mesh=mesh, in_specs=in_specs, out_specs=out_specs, check_vma=False
    )
```

profile of v0, /device:TPU:0, one launch (start us, length us, event | category | flops | bytes accessed | tf_op | source)
XLA Modules:
  0.0 1564.9 jit_solution(9987051581088941155)
XLA Ops:
  19.2 70.7 %all-gather.6.cloned.1.call-done = bf16[1536,2560]{1,0:T(8,128)(2,1)} async-done(((bf16[48,2560]{1,0:T(8,128)(2,1)}), bf16[1536,2560]{1,0:T(8,128)(2,1)}) %all-gather.6.cloned.1.call-update) | async-done | bytes 7864336 | tf_op jit(solution)/shard_map/all_gather | solution.py:158
  104.8 20.6 %all-gather.8.cloned.1.call-done = bf16[1024,1024]{1,0:T(8,128)(2,1)} async-done(((bf16[128,1024]{1,0:T(8,128)(2,1)}), bf16[1024,1024]{1,0:T(8,128)(2,1)}) %all-gather.8.cloned.1.call-update) | async-done | bytes 2097168 | tf_op jit(solution)/shard_map/all_gather | solution.py:175
  129.5 26.3 %while.28 = (s32[]{:T(128)}, f32[8,3,128]{2,1,0:T(4,128)S(1)}, f32[8,3,128]{2,1,0:T(4,128)S(1)}, f32[8,3,128,64]{2,3,1,0:T(8,128)S(1)}, s32[128]{0:T(128)}, /*in...) while((s32[]{:T(128)}, f32[8,3,128]{2,1,0:T(4,128)S(1)}, ...), condition=%wide.region_11.12_spmd.clone, body=%wide.region_8.11_spmd.clone.sunk | while | flops 423902336 | bytes 51721904 | solution.py:216
  136.2 4.5 fusion.137
  155.9 36.3 %all-gather.10.cloned.1.call-done = bf16[1536,1536]{1,0:T(8,128)(2,1)} async-done(((bf16[48,1536]{1,0:T(8,128)(2,1)}), bf16[1536,1536]{1,0:T(8,128)(2,1)}) %all-gather.10.cloned.1.call-update) | async-done | bytes 4718608 | tf_op jit(solution)/shard_map/all_gather | solution.py:159
  196.5 235.8 %all-gather.12.cloned.1.call-done = bf16[1536,13824]{1,0:T(8,128)(2,1)} async-done(((bf16[48,13824]{1,0:T(8,128)(2,1)}), bf16[1536,13824]{1,0:T(8,128)(2,1)}) %all-gather.12.cloned.1.call-update) | async-done | bytes 42467344 | tf_op jit(solution)/shard_map/all_gather | solution.py:228
  432.3 19.5 %fusion.74 = f32[128,13824]{1,0:T(8,128)} fusion(bf16[128,1536]{1,0:T(8,128)(2,1)S(1)} %multiply_convert_fusion.4, bf16[1536,13824]{1,0:T(8,128)(2,1)} %all-gather.12.cloned.1.call-done), kind=kOutput, calls=%fused_computation.172 | convolution fusion | flops 5435817984 | bytes 49938432 | tf_op jit(solution)/shard_map/dot_general | solution.py:226
  451.8 118.0 %all-gather.14.cloned.1.call-done = bf16[6912,1536]{1,0:T(8,128)(2,1)} async-done(((bf16[216,1536]{1,0:T(8,128)(2,1)}), bf16[6912,1536]{1,0:T(8,128)(2,1)}) %all-gather.14.cloned.1.call-update) | async-done | bytes 21233680 | tf_op jit(solution)/shard_map/all_gather | solution.py:239
  569.8 14.1 multiply_convert_fusion.1
  583.9 20.7 %multiply_reduce_fusion.1 = (f32[1536]{0:T(1024)}, f32[128]{0:T(128)}, f32[128,1536]{1,0:T(8,128)}) fusion(f32[128,1536]{1,0:T(8,128)} %copy-done.8, f32[128]{0:T(128)S(1)} %add_rsqrt_fusion.2, f32[1536]{0:T(1024)S(1)} %copy-done.55, bf16[1536,13824]{1,0:T(8,128)(2,1)} %all-gather.12.cloned.1.call-done, bf16[128,6912]{1,0:T(8,128)(2,1)} %get-tuple-element.381, ...), kind=kOutput, calls=%fused_computation.86 | convolution fusion | flops 5444073984 | bytes 47592448 | tf_op jit(solution)/shard_map/dot_general | solution.py:81
  614.3 35.8 %while.29 = (s32[]{:T(128)}, f32[8,3,128,64]{2,3,1,0:T(8,128)}, bf16[2,512,1024]{1,2,0:T(8,128)(2,1)}, s32[128]{0:T(128)}, s32[2,512]{1,0:T(2,128)}, /*index=5*/...) while((s32[]{:T(128)}, f32[8,3,128,64]{2,3,1,0:T(8,128)}, ...), condition=%wide.region_16.17_spmd.clone, body=%wide.region_15.16_spmd.clone.sunk | while | flops 1028915328 | bytes 85329824 | solution.py:291
  656.3 10.1 convolution_convert_fusion.1
  683.2 6.7 copy.134
  692.2 19.3 %convolution_convert_fusion = bf16[1536,13824]{1,0:T(8,128)(2,1)} fusion(bf16[128,1536]{0,1:T(8,128)(2,1)S(1)} %bitcast.257, bf16[128,6912]{1,0:T(8,128)(2,1)} %get-tuple-element.381, bf16[128,6912]{1,0:T(8,128)(2,1)} %get-tuple-element.380), kind=kOutput, calls=%fused_computation.47 | convolution fusion | flops 5464129536 | bytes 46399488 | tf_op jit(solution)/shard_map/dot_general | solution.py:75
  719.7 5.3 convolution_convert_fusion.2
  725.0 36.9 %pad_maximum_fusion = bf16[1536,17920]{1,0:T(8,128)(2,1)} fusion(bf16[1536,13824]{1,0:T(8,128)(2,1)} %convolution_convert_fusion, bf16[1536,1536]{1,0:T(8,128)(2,1)} %copy.134, bf16[1536,2560]{1,0:T(8,128)(2,1)} %convolution_convert_fusion.2), kind=kLoop, calls=%fused_computation.46 | loop fusion | flops 165150720 | bytes 110100480 | tf_op jit(solution)/shard_map/concatenate | solution.py:325
  762.0 137.5 %reduce-scatter.14.cloned.1.call-done = bf16[864,1536]{1,0:T(8,128)(2,1)} async-done(((bf16[6912,1536]{1,0:T(8,128)(2,1)}), bf16[864,1536]{1,0:T(8,128)(2,1)}) %reduce-scatter.14.cloned.1.call-update) | async-done | bytes 2654224 | tf_op jit(solution)/shard_map/reduce_scatter | solution.py:357
  899.8 528.1 %reduce-scatter.10.cloned.1.call-done = bf16[192,17920]{1,0:T(8,128)(2,1)} async-done(((bf16[1536,17920]{1,0:T(8,128)(2,1)}), bf16[192,17920]{1,0:T(8,128)(2,1)}) %reduce-scatter.10.cloned.1.call-update) | async-done | bytes 6881296 | tf_op jit(solution)/shard_map/reduce_scatter | solution.py:351
  1428.1 10.7 fusion.33
  1439.0 6.4 fusion.46
  1445.5 38.0 %psum.7 = f32[3200]{0:T(1024)S(1)} all-reduce(f32[3200]{0:T(1024)S(1)} %concatenate.57), channel_id=1, replica_groups=mesh['dp'=4,'cp'=8] {'dp','cp'}, use_global_device_ids=true, to_apply=%region_31.32 | all-reduce | flops 3200 | bytes 25600 | tf_op jit(solution)/shard_map/psum | solution.py:367
  1485.4 4.6 multiply_subtract_fusion.1
  1490.0 57.9 %reduce-scatter.12.cloned.1.call-done = bf16[48,17920]{1,0:T(8,128)(2,1)} async-done(((bf16[192,17920]{1,0:T(8,128)(2,1)}), bf16[48,17920]{1,0:T(8,128)(2,1)}) %reduce-scatter.12.cloned.1.call-update) | async-done | bytes 1720336 | tf_op jit(solution)/shard_map/reduce_scatter | solution.py:364
  1553.3 4.6 multiply_subtract_fusion
  (347 shorter events, 142.0 us)
Async XLA Ops:
  7.2 82.7 %all-gather.6.cloned.1.call-start = ((), (), s32[]{:S(2)}) async-start(), calls=%async_computation.5 | async-start | bytes 8110080 | tf_op jit(solution)/shard_map/all_gather | solution.py:158
  9.0 116.4 %all-gather.8.cloned.1.call-start = ((), (), s32[]{:S(2)}) async-start(), calls=%async_computation.6 | async-start | bytes 2359296 | tf_op jit(solution)/shard_map/all_gather | solution.py:175
  15.0 79.3 %copy-start.71 = (f32[128]{0:T(128)}, f32[128]{0:T(128)S(1)}, u32[]{:S(2)}) copy-start(f32[128]{0:T(128)S(1)} %add_rsqrt_fusion.3) | copy-start | bytes 1540
  15.9 79.8 %copy-start.67 = (f32[64]{0:T(128)}, f32[64]{0:T(128)S(1)}, u32[]{:S(2)}) copy-start(f32[64]{0:T(128)S(1)} %get-tuple-element.404) | copy-start | bytes 772
  15.9 88.2 %copy-start.69 = (f32[64]{0:T(128)}, f32[64]{0:T(128)S(1)}, u32[]{:S(2)}) copy-start(f32[64]{0:T(128)S(1)} %get-tuple-element.403) | copy-start | bytes 772
  17.2 77.0 %copy-start.53 = (f32[1536]{0:T(1024)}, f32[1536]{0:T(1024)S(1)}, u32[]{:S(2)}) copy-start(f32[1536]{0:T(1024)S(1)} %get-tuple-element.402) | copy-start | bytes 18436
  18.0 86.2 %copy-start.47 = (f32[128,32]{0,1:T(8,128)}, f32[128,32]{0,1:T(8,128)S(1)}, u32[]{:S(2)}) copy-start(f32[128,32]{0,1:T(8,128)S(1)} %get-tuple-element.407) | copy-start | bytes 49156
  19.2 70.7 %copy-start.19 = (bf16[128,1536]{1,0:T(8,128)(2,1)}, bf16[128,1536]{1,0:T(8,128)(2,1)S(1)}, u32[]{:S(2)}) copy-start(bf16[128,1536]{1,0:T(8,128)(2,1)S(1)} %fusion.41) | copy-start | bytes 1179652
  97.6 94.6 %all-gather.10.cloned.1.call-start = ((), (), s32[]{:S(2)}) async-start(), calls=%async_computation.7 | async-start | bytes 4866048 | tf_op jit(solution)/shard_map/all_gather | solution.py:159
  98.4 333.9 %all-gather.12.cloned.1.call-start = ((), (), s32[]{:S(2)}) async-start(), calls=%async_computation.8 | async-start | bytes 43794432 | tf_op jit(solution)/shard_map/all_gather | solution.py:228
  99.6 470.2 %all-gather.14.cloned.1.call-start = ((), (), s32[]{:S(2)}) async-start(), calls=%async_computation.9 | async-start | bytes 21897216 | tf_op jit(solution)/shard_map/all_gather | solution.py:239
  102.0 609.5 %reduce-scatter.8.cloned.1.call-start = ((), (), s32[]{:S(2)}) async-start(), calls=%async_computation.10 | async-start | bytes 2359296 | tf_op jit(solution)/shard_map/reduce_scatter | solution.py:296
  129.5 62.7 %copy-start.16 = (bf16[128,1536]{1,0:T(8,128)(2,1)S(1)}, bf16[128,1536]{1,0:T(8,128)(2,1)}, u32[]{:S(2)}) copy-start(bf16[128,1536]{1,0:T(8,128)(2,1)} %param.23) | copy-start | bytes 1179652
  196.5 255.4 %copy-start.23 = (bf16[128,1536]{1,0:T(8,128)(2,1)}, bf16[128,1536]{1,0:T(8,128)(2,1)S(1)}, u32[]{:S(2)}) copy-start(bf16[128,1536]{1,0:T(8,128)(2,1)S(1)} %multiply_convert_fusion.4) | copy-start | bytes 1179652
  196.5 373.4 %copy-start.36 = (bf16[128,1536]{1,0:T(8,128)(2,1)S(1)}, bf16[128,1536]{1,0:T(8,128)(2,1)}, u32[]{:S(2)}) copy-start(bf16[128,1536]{1,0:T(8,128)(2,1)} %param.24) | copy-start | bytes 1179652
  654.2 245.4 %reduce-scatter.14.cloned.1.call-start = ((), (), s32[]{:S(2)}) async-start(), calls=%async_computation.13 | async-start | bytes 23887872 | tf_op jit(solution)/shard_map/reduce_scatter | solution.py:357
  666.5 761.4 %reduce-scatter.10.cloned.1.call-start = ((), (), s32[]{:S(2)}) async-start(), calls=%async_computation.11 | async-start | bytes 61931520 | tf_op jit(solution)/shard_map/reduce_scatter | solution.py:351
  762.0 723.4 %reduce-scatter.16.cloned.1.call-start = ((), (), s32[]{:S(2)}) async-start(), calls=%async_computation.14 | async-start | bytes 3317760
  899.6 528.3 %copy-start.59 = (f32[1536]{0:T(1024)S(1)}, f32[1536]{0:T(1024)}, u32[]{:S(2)}) copy-start(f32[1536]{0:T(1024)} %get-tuple-element.383) | copy-start | bytes 18436
  899.6 528.4 %copy-start.9 = (f32[128,1536]{1,0:T(8,128)S(1)}, f32[128,1536]{1,0:T(8,128)}, u32[]{:S(2)}) copy-start(f32[128,1536]{1,0:T(8,128)} %copy-done.8) | copy-start | bytes 2359300
  899.6 528.4 %copy-start.15 = (bf16[128,6912]{1,0:T(8,128)(2,1)S(1)}, bf16[128,6912]{1,0:T(8,128)(2,1)}, u32[]{:S(2)}) copy-start(bf16[128,6912]{1,0:T(8,128)(2,1)} %get-tuple-element.382) | copy-start | bytes 5308420
  899.6 648.3 %reduce-scatter.12.cloned.1.call-start = ((), (), s32[]{:S(2)}) async-start(), calls=%async_computation.12 | async-start | bytes 8601600 | tf_op jit(solution)/shard_map/reduce_scatter | solution.py:364
  1490.0 61.2 %copy-start.41 = (f32[48,1536]{1,0:T(8,128)S(1)}, f32[48,1536]{1,0:T(8,128)}, u32[]{:S(2)}) copy-start(f32[48,1536]{1,0:T(8,128)} %param.30) | copy-start | bytes 884740
  1490.0 61.2 %copy-start.49 = (f32[48,1536]{1,0:T(8,128)S(1)}, f32[48,1536]{1,0:T(8,128)}, u32[]{:S(2)}) copy-start(f32[48,1536]{1,0:T(8,128)} %param.31) | copy-start | bytes 884740
  (75 other events, 939.6 us)
Sparse Core Ops, SparseCore 0:
  11.6 78.1 all-gather.5
  97.7 27.6 all-gather.7
  129.0 63.1 all-gather.9
  195.6 236.5 all-gather.11
  435.7 134.0 all-gather.13
  654.3 34.0 reduce-scatter.7
  690.7 208.7 reduce-scatter.13
  902.1 525.7 reduce-scatter.9
  1430.9 38.7 reduce-scatter.15
  1472.6 75.2 reduce-scatter.11
where the time goes:
time: 1570 us; the launch traced here: 1560 us
  waiting for transfers between devices  1210 us (77%)
  matrix products  157 us (10%)
  other arithmetic  96.5 us (6%)
  local copies, waits for them, and re-layouts  51.1 us (3%)
  blocking collectives  38 us (2%)
  between operations  16 us (1%)
    reduce_scatter x1, waiting for transfers between devices, on_device(): lax.psum_scatter(wide_fn(jnp.int32(0), lax.axis_size('cp') * (shard_rows...  528 us
    all_gather x1, waiting for transfers between devices, on_device(): lax.all_gather(gateup_bf, ('dp', 'cp'), axis=0, tiled=True)  236 us
    reduce_scatter x1, waiting for transfers between devices, on_device(): lax.psum_scatter(down_fn(jnp.int32(0), lax.axis_size('cp') * (down_rows *...  138 us
    all_gather x1, waiting for transfers between devices, on_device(): lax.all_gather(down_bf, ('dp', 'cp'), axis=0, tiled=True)  118 us
    all_gather x1, waiting for transfers between devices, on_device(): lax.all_gather(input_bf, ('dp', 'cp'), axis=0, tiled=True)  70.7 us
    reduce_scatter x1, waiting for transfers between devices, on_device(): lax.psum_scatter(group_wide, 'dp', scatter_dimension=0, tiled=True)  57.9 us
    dot_general x4, matrix products, contract_cols(): lax.dot_general(left, right, (((1,), (1,)), ((), ())), preferred_element_...  43.6 us
    dot_general x4, matrix products, contract_rows(): lax.dot_general(left, right, (((0,), (0,)), ((), ())), preferred_element_...  38.3 us
  transfers between devices with their start and end apart: 10, of which 8 were waited for; matrix products, arithmetic and copies ran while one was open for 13% of the time, Pallas kernels for 0%

commit v1 on v0

--- a/solution.py
+++ b/solution.py
@@ -1,8 +1,11 @@
+import functools
 import math
 
 import jax
 import jax.numpy as jnp
 from jax import lax
+from jax.experimental import pallas as pl
+from jax.experimental.pallas import tpu as pltpu
 from jax.sharding import PartitionSpec as P
 
 HEADS = 24
@@ -407,6 +410,1033 @@
     )
 
 
+MESH = pl.DeviceIdType.MESH
+
+
+def place():
+    dp = lax.axis_index("dp")
+    cp = lax.axis_index("cp")
+    return dp, cp, cp // 2, cp % 2
+
+
+def greet(targets):
+    barrier = pltpu.get_barrier_semaphore()
+    for target in targets:
+        pl.semaphore_signal(barrier, inc=1, device_id=target, device_id_type=MESH)
+    pl.semaphore_wait(barrier, len(targets))
+
+
+def send(source, target, send_sem, recv_sem, device):
+    return pltpu.make_async_remote_copy(
+        src_ref=source,
+        dst_ref=target,
+        send_sem=send_sem,
+        recv_sem=recv_sem,
+        device_id=device,
+        device_id_type=MESH,
+    )
+
+
+class LineGather:
+    def __init__(self, own_ref, all_ref, sems, where, depth, both=True):
+        self.own, self.where, self.depth, self.both = own_ref, where, depth, both
+        self.slot = all_ref if callable(all_ref) else lambda slot: all_ref.at[slot]
+        self.right, self.left, self.sib, self.recv, self.local = sems
+
+    @staticmethod
+    def scratch(depth):
+        return [pltpu.SemaphoreType.DMA((2 * depth,))] * 4 + [pltpu.SemaphoreType.DMA]
+
+    def copy(self, kind, slot, source):
+        dp, cp, z, core = self.where
+        device = {"right": (dp, cp + 2), "left": (dp, cp - 2), "sib": (dp, cp ^ 1)}[kind]
+        sem = {"right": self.right, "left": self.left, "sib": self.sib}[kind]
+        return send(source, self.slot(slot), sem.at[slot], self.recv.at[slot], device)
+
+    def keep(self):
+        return pltpu.make_async_copy(self.own, self.slot(self.where[1]), self.local)
+
+    def start(self):
+        dp, cp, z, core = self.where
+
+        @pl.when(z < self.depth - 1)
+        def _():
+            self.copy("right", cp, self.own).start()
+
+        @pl.when(z > 0)
+        def _():
+            self.copy("left", cp, self.own).start()
+
+        if self.both:
+            self.copy("sib", cp, self.own).start()
+        self.keep().start()
+
+    def step(self, far):
+        dp, cp, z, core = self.where
+
+        @pl.when(z >= far)
+        def _():
+            slot = cp - 2 * far
+            self.copy("right", slot, self.own).wait_recv()
+
+            @pl.when(z < self.depth - 1)
+            def _():
+                self.copy("right", slot, self.slot(slot)).start()
+
+            if self.both:
+                self.copy("sib", slot, self.slot(slot)).start()
+
+        @pl.when(z + far < self.depth)
+        def _():
+            slot = cp + 2 * far
+            self.copy("left", slot, self.own).wait_recv()
+
+            @pl.when(z > 0)
+            def _():
+                self.copy("left", slot, self.slot(slot)).start()
+
+            if self.both:
+                self.copy("sib", slot, self.slot(slot)).start()
+
+    def finish(self):
+        dp, cp, z, core = self.where
+        if self.both:
+            for spot in range(self.depth):
+                self.copy("sib", 1 - core + 2 * spot, self.own).wait_recv()
+        self.keep().wait()
+        for spot in range(self.depth):
+            slot = 2 * spot + core
+            if self.both:
+                self.copy("sib", slot, self.own).wait_send()
+
+            @pl.when((spot <= z) & (z < self.depth - 1))
+            def _():
+                self.copy("right", slot, self.own).wait_send()
+
+            @pl.when((spot >= z) & (z > 0))
+            def _():
+                self.copy("left", slot, self.own).wait_send()
+
+
+class Swap:
+    def __init__(self, source_ref, target_ref, sems, where, count):
+        self.source, self.where, self.count = source_ref, where, count
+        self.slot = target_ref if callable(target_ref) else lambda slot: target_ref.at[slot]
+        self.sent, self.recv, self.local = sems
+
+    @staticmethod
+    def scratch(count):
+        return [pltpu.SemaphoreType.DMA((count,))] * 2 + [pltpu.SemaphoreType.DMA]
+
+    def copy(self, peer):
+        dp, cp, z, core = self.where
+        return send(
+            self.source.at[peer],
+            self.slot(cp),
+            self.sent.at[peer],
+            self.recv.at[cp],
+            (dp, peer),
+        )
+
+    def keep(self):
+        cp = self.where[1]
+        return pltpu.make_async_copy(self.source.at[cp], self.slot(cp), self.local)
+
+    def start(self):
+        cp = self.where[1]
+        for turn in range(self.count - 1, 0, -1):
+            self.copy(cp ^ turn).start()
+        self.keep().start()
+
+    def arrive(self, peer):
+        dp, cp, z, core = self.where
+        send(
+            self.source.at[peer],
+            self.slot(peer),
+            self.sent.at[peer],
+            self.recv.at[peer],
+            (dp, peer),
+        ).wait_recv()
+
+    def finish_recv(self):
+        cp = self.where[1]
+        for turn in range(1, self.count):
+            self.arrive(cp ^ turn)
+        self.keep().wait()
+
+    def finish_send(self):
+        cp = self.where[1]
+        for turn in range(1, self.count):
+            self.copy(cp ^ turn).wait_send()
+
+
+class RingSpread:
+    def __init__(self, block, half, sems, where):
+        self.block, self.half, self.where = block, half, where
+        self.sent, self.recv = sems
+
+    @staticmethod
+    def scratch():
+        return [pltpu.SemaphoreType.DMA((4,))] * 2
+
+    def copy(self, kind, mine):
+        dp, cp, z, core = self.where
+        turn = (1, 2, 2, 1)[kind]
+        if kind < 2:
+            part = self.block(dp if mine else dp ^ turn)
+        else:
+            part = self.half(dp ^ (3 - turn) if mine else dp ^ 3, kind - 2)
+        return send(part, part, self.sent.at[kind], self.recv.at[kind], (dp ^ turn, cp))
+
+    def start(self):
+        self.copy(0, True).start()
+        self.copy(1, True).start()
+
+    def forward(self):
+        self.copy(0, False).wait_recv()
+        self.copy(2, True).start()
+        self.copy(1, False).wait_recv()
+        self.copy(3, True).start()
+
+    def finish(self):
+        self.copy(2, False).wait_recv()
+        self.copy(3, False).wait_recv()
+        for kind in range(4):
+            self.copy(kind, True).wait_send()
+
+
+def turn_heads(values, cosine, sine):
+    half = values.shape[0] // 2
+    first, second = values[:half], values[half:]
+    return jnp.concatenate([first * cosine - second * sine, second * cosine + first * sine], axis=0)
+
+
+def head_hat(values):
+    inverse = lax.rsqrt(jnp.mean(values * values, axis=0, keepdims=True) + norm_eps)
+    return values * inverse, inverse
+
+
+def score_block(keys, queries, key_place, query_place, query_start):
+    scores = jnp.dot(keys, queries, preferred_element_type=jnp.float32) * HEAD_DIM ** (-0.5)
+    allowed = (key_place <= query_place) & (key_place >= query_start)
+    return jnp.where(allowed, scores, masked_score), allowed
+
+
+def front_kernel(
+    tile,
+    tokens_ref,
+    gain_one_ref,
+    gain_two_ref,
+    gain_query_ref,
+    gain_key_ref,
+    cosine_ref,
+    sine_ref,
+    key_place_ref,
+    query_place_ref,
+    query_start_ref,
+    input_send,
+    output_own,
+    gate_send,
+    up_send,
+    cotangent_own,
+    normed_one_out,
+    normed_two_out,
+    cotangent_all,
+    input_out,
+    output_out,
+    gateup_out,
+    raw_out,
+    flat_out,
+    total_out,
+    residual_out,
+    normed_one,
+    normed_two,
+    own_one,
+    own_two,
+    inputs,
+    outputs,
+    raw,
+    queries,
+    keys_up,
+    values,
+    flat_send,
+    flat_recv,
+    out_sems,
+    *sems,
+):
+    where = place()
+    dp, cp, z, core = where
+    context_count = normed_one.shape[0]
+    depth = context_count // 2
+    rows = tokens_ref.shape[0]
+    width = tokens_ref.shape[1]
+    q_each = HEADS // KV_HEADS * HEAD_DIM
+    take = iter(range(len(sems)))
+
+    def some(count):
+        return [sems[next(take)] for _ in range(count)]
+
+    greet([(dp, cp ^ turn) for turn in range(1, context_count)] + [(dp ^ 1, cp), (dp ^ 2, cp)])
+    token_line = LineGather(own_one, normed_one, some(5), where, depth)
+    second_line = LineGather(own_two, normed_two, some(5), where, depth)
+    cotangent_line = LineGather(cotangent_own, cotangent_all, some(5), where, depth)
+    output_line = LineGather(
+        output_own, lambda slot: outputs.at[dp, slot // 2, core], some(5), where, depth, False
+    )
+    input_swap = Swap(input_send, inputs.at[dp], some(3), where, context_count)
+    shard = input_send.shape[1]
+
+    def gateup_slot(index):
+        return lambda slot: gateup_out.at[index, dp, pl.ds(pl.multiple_of(slot * shard, 16), shard)]
+
+    gate_swap = Swap(gate_send, gateup_slot(0), some(3), where, context_count)
+    up_swap = Swap(up_send, gateup_slot(1), some(3), where, context_count)
+    flat_swap = Swap(flat_send, flat_recv, some(3), where, context_count)
+    input_ring = RingSpread(
+        lambda d: inputs.at[d],
+        lambda d, h: inputs.at[d, pl.ds(h * (context_count // 2), context_count // 2)],
+        some(2),
+        where,
+    )
+    output_ring = RingSpread(
+        lambda d: outputs.at[d, :, core],
+        lambda d, h: outputs.at[d, pl.ds(h * (depth // 2), depth // 2), core],
+        some(2),
+        where,
+    )
+    half_rows = gateup_out.shape[2] // 2
+
+    def gateup_ring(index):
+        return RingSpread(
+            lambda d: gateup_out.at[index, d],
+            lambda d, h: gateup_out.at[index, d, pl.ds(h * half_rows, half_rows)],
+            some(2),
+            where,
+        )
+
+    gate_ring, up_ring = gateup_ring(0), gateup_ring(1)
+    share_sent, share_recv = some(2)
+
+    def share(mine):
+        part = outputs.at[:, :, core if mine else 1 - core]
+        return send(part, part, share_sent, share_recv, (dp, cp ^ 1))
+
+    x_float = tokens_ref[...].astype(jnp.float32)
+    hat_one, _ = rms_parts(x_float)
+    own_one[...] = (hat_one * gain_one_ref[...]).astype(jnp.bfloat16)
+    input_swap.start()
+    token_line.start()
+    output_line.start()
+    token_line.step(1)
+    output_line.step(1)
+    input_swap.finish_recv()
+    input_ring.start()
+    token_line.step(2)
+    output_line.step(2)
+    gate_swap.start()
+    input_ring.forward()
+    token_line.step(3)
+    output_line.step(3)
+    up_swap.start()
+    output_line.finish()
+    output_ring.start()
+    token_line.finish()
+    input_ring.finish()
+    one_copy = pltpu.make_async_copy(normed_one, normed_one_out, out_sems.at[0])
+    one_copy.start()
+    input_copy = pltpu.make_async_copy(inputs, input_out, out_sems.at[1])
+    input_copy.start()
+
+    weights = inputs[...].reshape(width, inputs.shape[-1])
+
+    def project(turn, carry):
+        lanes = pl.ds(pl.multiple_of(turn * tile, tile), tile)
+        block = normed_one[pl.ds(turn * (tile // rows), tile // rows)].reshape(tile, width)
+        part = jnp.dot(block, weights, preferred_element_type=jnp.float32).T
+        raw[:, lanes] = part
+        cosine, sine = cosine_ref[:, lanes], sine_ref[:, lanes]
+        for head in range(HEADS // KV_HEADS):
+            hat, _ = head_hat(part[head * HEAD_DIM : (head + 1) * HEAD_DIM])
+            queries[head * HEAD_DIM : (head + 1) * HEAD_DIM, lanes] = turn_heads(
+                hat * gain_query_ref[...], cosine, sine
+            ).astype(jnp.bfloat16)
+        hat, _ = head_hat(part[q_each : q_each + HEAD_DIM])
+        key = turn_heads(hat * gain_key_ref[...], cosine, sine)
+        keys_up[pl.ds(pl.multiple_of(turn * tile, tile), tile)] = key.T.astype(jnp.bfloat16)
+        values[:, lanes] = part[q_each + HEAD_DIM :].astype(jnp.bfloat16)
+        return carry
+
+    lax.fori_loop(0, normed_one.shape[0] * rows // tile, project, 0)
+    raw_copy = pltpu.make_async_copy(raw, raw_out, out_sems.at[2])
+    raw_copy.start()
+
+    def attend(turn, carry):
+        lanes = pl.ds(pl.multiple_of(turn * tile, tile), tile)
+        query_place, query_start = query_place_ref[:, lanes], query_start_ref[:, lanes]
+        for head in range(HEADS // KV_HEADS):
+            spot = pl.ds(head * HEAD_DIM, HEAD_DIM)
+            scores, allowed = score_block(
+                keys_up[...], queries[spot, lanes], key_place_ref[...], query_place, query_start
+            )
+            top = jnp.max(scores, axis=0, keepdims=True)
+            exps = jnp.exp(scores - top)
+            total = jnp.sum(exps, axis=0, keepdims=True)
+            total_out[pl.ds(head, 1), lanes] = top + jnp.log(total)
+            probs = (exps * (1.0 / total)).astype(jnp.bfloat16)
+            attended = jnp.dot(values[...], probs, preferred_element_type=jnp.float32)
+            for part in range(tile // rows):
+                flat_send[turn * (tile // rows) + part, spot] = attended[
+                    :, part * rows : (part + 1) * rows
+                ].astype(jnp.bfloat16)
+        return carry
+
+    turns = normed_one.shape[0] * rows // tile
+    attend(0, 0)
+    gate_swap.finish_recv()
+    gate_ring.start()
+    output_ring.forward()
+    lax.fori_loop(1, turns, attend, 0)
+    flat_swap.start()
+    up_swap.finish_recv()
+    up_ring.start()
+    output_ring.finish()
+    share(True).start()
+    gate_ring.forward()
+    cotangent_line.start()
+    share(False).wait_recv()
+    output_copy = pltpu.make_async_copy(outputs, output_out, out_sems.at[3])
+    output_copy.start()
+    flat_swap.finish_recv()
+    flat_copy = pltpu.make_async_copy(flat_recv, flat_out, out_sems.at[4])
+    flat_copy.start()
+    flat = flat_recv[...].reshape(HEADS * HEAD_DIM, rows).astype(jnp.float32).T.astype(jnp.bfloat16)
+    residual = x_float + jnp.dot(
+        flat, outputs[...].reshape(HEADS * HEAD_DIM, width), preferred_element_type=jnp.float32
+    )
+    residual_out[...] = residual
+    hat_two, _ = rms_parts(residual)
+    own_two[...] = (hat_two * gain_two_ref[...]).astype(jnp.bfloat16)
+    second_line.start()
+    for far in range(1, depth):
+        second_line.step(far)
+        cotangent_line.step(far)
+        if far == 1:
+            up_ring.forward()
+    second_line.finish()
+    two_copy = pltpu.make_async_copy(normed_two, normed_two_out, out_sems.at[5])
+    two_copy.start()
+    cotangent_line.finish()
+    gate_ring.finish()
+    up_ring.finish()
+    share(True).wait_send()
+    for swap in (input_swap, gate_swap, up_swap, flat_swap):
+        swap.finish_send()
+    for copy in (one_copy, input_copy, raw_copy, output_copy, flat_copy, two_copy):
+        copy.wait()
+
+
+def front(
+    tokens,
+    gain_one,
+    gain_two,
+    gain_query,
+    gain_key,
+    cosine,
+    sine,
+    places,
+    starts,
+    input_send,
+    output_own,
+    gate_send,
+    up_send,
+    cotangent,
+    data_count,
+    context_count,
+):
+    rows, width = tokens.shape
+    depth = context_count // 2
+    group_rows = rows * context_count
+    shard = input_send.shape[1]
+    each = input_send.shape[2]
+    hidden = gate_send.shape[2]
+    q_each = HEADS // KV_HEADS * HEAD_DIM
+    flat_width = HEADS * HEAD_DIM
+    bf = jnp.bfloat16
+    any_space = pl.BlockSpec(memory_space=pl.ANY)
+    in_vmem = pl.BlockSpec(memory_space=pltpu.VMEM)
+    shapes = [
+        ((context_count, rows, width), bf, any_space),
+        ((context_count, rows, width), bf, any_space),
+        ((context_count, rows, width), bf, any_space),
+        ((data_count, context_count, shard, each), bf, any_space),
+        ((data_count, depth, 2, shard, width), bf, any_space),
+        ((2, data_count, context_count * shard, hidden), bf, any_space),
+        ((each, group_rows), jnp.float32, any_space),
+        ((context_count, q_each, rows), bf, any_space),
+        ((HEADS // KV_HEADS, group_rows), jnp.float32, in_vmem),
+        ((rows, width), jnp.float32, in_vmem),
+    ]
+    return pl.pallas_call(
+        functools.partial(front_kernel, 2 * rows),
+        out_shape=[jax.ShapeDtypeStruct(shape, kind) for shape, kind, _ in shapes],
+        in_specs=[in_vmem] * 10 + [any_space] * 5,
+        out_specs=[space for _, _, space in shapes],
+        scratch_shapes=[
+            pltpu.VMEM((context_count, rows, width), bf),
+            pltpu.VMEM((context_count, rows, width), bf),
+            pltpu.VMEM((rows, width), bf),
+            pltpu.VMEM((rows, width), bf),
+            pltpu.VMEM((data_count, context_count, shard, each), bf),
+            pltpu.VMEM((data_count, depth, 2, shard, width), bf),
+            pltpu.VMEM((each, group_rows), jnp.float32),
+            pltpu.VMEM((q_each, group_rows), bf),
+            pltpu.VMEM((group_rows, HEAD_DIM), bf),
+            pltpu.VMEM((HEAD_DIM, group_rows), bf),
+            pltpu.VMEM((context_count, q_each, rows), bf),
+            pltpu.VMEM((context_count, q_each, rows), bf),
+            pltpu.SemaphoreType.DMA((6,)),
+        ]
+        + LineGather.scratch(depth) * 4
+        + Swap.scratch(context_count) * 4
+        + RingSpread.scratch() * 4
+        + [pltpu.SemaphoreType.DMA] * 2,
+        compiler_params=pltpu.CompilerParams(
+            collective_id=0, has_side_effects=True, vmem_limit_bytes=56 * 2**20
+        ),
+        name="front",
+    )(
+        tokens,
+        gain_one.reshape(1, width),
+        gain_two.reshape(1, width),
+        gain_query.reshape(HEAD_DIM, 1),
+        gain_key.reshape(HEAD_DIM, 1),
+        cosine,
+        sine,
+        places.reshape(group_rows, 1),
+        places.reshape(1, group_rows),
+        starts.reshape(1, group_rows),
+        input_send,
+        output_own,
+        gate_send,
+        up_send,
+        cotangent,
+    )
+
+
+def swap_kernel(context_count, source_ref, target_ref, *sems):
+    where = place()
+    dp, cp, z, core = where
+    greet([(dp, cp ^ turn) for turn in range(1, context_count)])
+    swap = Swap(source_ref, target_ref, sems, where, context_count)
+    swap.start()
+    swap.finish_recv()
+    swap.finish_send()
+
+
+def swap_blocks(source, collective_id, name):
+    any_space = pl.BlockSpec(memory_space=pl.ANY)
+    return pl.pallas_call(
+        functools.partial(swap_kernel, source.shape[0]),
+        out_shape=jax.ShapeDtypeStruct(source.shape, source.dtype),
+        in_specs=[any_space],
+        out_specs=any_space,
+        scratch_shapes=Swap.scratch(source.shape[0]),
+        compiler_params=pltpu.CompilerParams(collective_id=collective_id, has_side_effects=True),
+        name=name,
+    )(source)
+
+
+def gather_kernel(depth, own_ref, all_ref, *sems):
+    where = place()
+    dp, cp, z, core = where
+    greet([(dp, cp ^ turn) for turn in range(1, 2 * depth)])
+    line = LineGather(own_ref, all_ref, sems, where, depth)
+    line.start()
+    for far in range(1, depth):
+        line.step(far)
+    line.finish()
+
+
+def gather_line(own, context_count, collective_id, name):
+    any_space = pl.BlockSpec(memory_space=pl.ANY)
+    depth = context_count // 2
+    return pl.pallas_call(
+        functools.partial(gather_kernel, depth),
+        out_shape=jax.ShapeDtypeStruct((context_count,) + own.shape, own.dtype),
+        in_specs=[any_space],
+        out_specs=any_space,
+        scratch_shapes=LineGather.scratch(depth),
+        compiler_params=pltpu.CompilerParams(collective_id=collective_id, has_side_effects=True),
+        name=name,
+    )(own)
+
+
+class LineScatter:
+    def __init__(self, part_ref, out_ref, scratch, where, depth):
+        self.part, self.out, self.where, self.depth = part_ref, out_ref, where, depth
+        self.sib, self.msg, self.right, self.left = scratch[:4]
+        (
+            self.sib_sent,
+            self.sib_recv,
+            self.right_sent,
+            self.right_recv,
+            self.left_sent,
+            self.left_recv,
+        ) = scratch[4:]
+
+    @staticmethod
+    def scratch(depth, rows, width):
+        return [pltpu.VMEM((depth, rows, width), jnp.bfloat16)] * 4 + [
+            pltpu.SemaphoreType.DMA((depth,))
+        ] * 6
+
+    def pair(self, spot):
+        dp, cp, z, core = self.where
+        return send(
+            self.part.at[2 * spot + 1 - core],
+            self.sib.at[spot],
+            self.sib_sent.at[spot],
+            self.sib_recv.at[spot],
+            (dp, cp ^ 1),
+        )
+
+    def hop_right(self, spot):
+        dp, cp, z, core = self.where
+        return send(
+            self.msg.at[spot],
+            self.right.at[spot],
+            self.right_sent.at[spot],
+            self.right_recv.at[spot],
+            (dp, cp + 2),
+        )
+
+    def hop_left(self, spot):
+        dp, cp, z, core = self.where
+        return send(
+            self.msg.at[spot],
+            self.left.at[spot],
+            self.left_sent.at[spot],
+            self.left_recv.at[spot],
+            (dp, cp - 2),
+        )
+
+    def order(self):
+        spots = []
+        for turn in range(self.depth):
+            spots += [self.depth - 1 - turn, turn]
+        return list(dict.fromkeys(spots))
+
+    def chip_sum(self, spot):
+        core = self.where[3]
+        self.pair(spot).wait_recv()
+        return self.part[2 * spot + core].astype(jnp.float32) + self.sib[spot].astype(jnp.float32)
+
+    def forward(self, spot):
+        z = self.where[2]
+
+        @pl.when((z < spot) & (z > 0))
+        def _():
+            total = self.chip_sum(spot)
+            self.hop_right(spot).wait_recv()
+            self.msg[spot] = (total + self.right[spot].astype(jnp.float32)).astype(jnp.bfloat16)
+            self.hop_right(spot).start()
+
+        @pl.when((z < spot) & (z == 0))
+        def _():
+            self.msg[spot] = self.chip_sum(spot).astype(jnp.bfloat16)
+            self.hop_right(spot).start()
+
+        @pl.when((z > spot) & (z < self.depth - 1))
+        def _():
+            total = self.chip_sum(spot)
+            self.hop_left(spot).wait_recv()
+            self.msg[spot] = (total + self.left[spot].astype(jnp.float32)).astype(jnp.bfloat16)
+            self.hop_left(spot).start()
+
+        @pl.when((z > spot) & (z == self.depth - 1))
+        def _():
+            self.msg[spot] = self.chip_sum(spot).astype(jnp.bfloat16)
+            self.hop_left(spot).start()
+
+    def finish(self):
+        z = self.where[2]
+        self.out[...] = self.chip_sum(z)
+
+        @pl.when(z > 0)
+        def _():
+            self.hop_right(z).wait_recv()
+            self.out[...] += self.right[z].astype(jnp.float32)
+
+        @pl.when(z < self.depth - 1)
+        def _():
+            self.hop_left(z).wait_recv()
+            self.out[...] += self.left[z].astype(jnp.float32)
+
+        for spot in range(self.depth):
+            self.pair(spot).wait_send()
+
+            @pl.when(z < spot)
+            def _():
+                self.hop_right(spot).wait_send()
+
+            @pl.when(z > spot)
+            def _():
+                self.hop_left(spot).wait_send()
+
+
+def scatter_kernel(depth, part_ref, out_ref, *scratch):
+    where = place()
+    dp, cp, z, core = where
+    greet([(dp, cp ^ turn) for turn in range(1, 2 * depth)])
+    line = LineScatter(part_ref, out_ref, scratch, where, depth)
+    for spot in line.order():
+        line.pair(spot).start()
+    for spot in line.order():
+        line.forward(spot)
+    line.finish()
+
+
+def scatter_line(parts, collective_id, name):
+    context_count, rows, width = parts.shape
+    depth = context_count // 2
+    in_vmem = pl.BlockSpec(memory_space=pltpu.VMEM)
+    return pl.pallas_call(
+        functools.partial(scatter_kernel, depth),
+        out_shape=jax.ShapeDtypeStruct((rows, width), jnp.float32),
+        in_specs=[in_vmem],
+        out_specs=in_vmem,
+        scratch_shapes=LineScatter.scratch(depth, rows, width),
+        compiler_params=pltpu.CompilerParams(
+            collective_id=collective_id, has_side_effects=True, vmem_limit_bytes=40 * 2**20
+        ),
+        name=name,
+    )(parts)
+
+
+def total_kernel(data_count, context_count, own_ref, out_ref, line_buf, all_buf, *sems):
+    where = place()
+    dp, cp, z, core = where
+    line_sent, line_recv, all_sent, all_recv = sems
+    greet(
+        [(dp, cp ^ turn) for turn in range(1, context_count)]
+        + [(dp ^ turn, cp) for turn in range(1, data_count)]
+    )
+    line_buf[cp] = own_ref[...]
+    for turn in range(1, context_count):
+        send(
+            own_ref, line_buf.at[cp], line_sent.at[turn], line_recv.at[turn], (dp, cp ^ turn)
+        ).start()
+    for turn in range(1, context_count):
+        copy = send(
+            own_ref, line_buf.at[cp ^ turn], line_sent.at[turn], line_recv.at[turn], (dp, cp ^ turn)
+        )
+        copy.wait_recv()
+        copy.wait_send()
+    all_buf[dp] = jnp.sum(line_buf[...], axis=0)
+    for turn in range(1, data_count):
+        send(
+            all_buf.at[dp], all_buf.at[dp], all_sent.at[turn], all_recv.at[turn], (dp ^ turn, cp)
+        ).start()
+    for turn in range(1, data_count):
+        copy = send(
+            all_buf.at[dp], all_buf.at[dp ^ turn], all_sent.at[turn], all_recv.at[turn], (dp ^ turn, cp)
+        )
+        copy.wait_recv()
+        copy.wait_send()
+    out_ref[...] = jnp.sum(all_buf[...], axis=0)
+
+
+def total_everywhere(own, data_count, context_count, collective_id):
+    in_vmem = pl.BlockSpec(memory_space=pltpu.VMEM)
+    return pl.pallas_call(
+        functools.partial(total_kernel, data_count, context_count),
+        out_shape=jax.ShapeDtypeStruct(own.shape, jnp.float32),
+        in_specs=[in_vmem],
+        out_specs=in_vmem,
+        scratch_shapes=[
+            pltpu.VMEM((context_count,) + own.shape, jnp.float32),
+            pltpu.VMEM((data_count,) + own.shape, jnp.float32),
+            pltpu.SemaphoreType.DMA((context_count,)),
+            pltpu.SemaphoreType.DMA((context_count,)),
+            pltpu.SemaphoreType.DMA((data_count,)),
+            pltpu.SemaphoreType.DMA((data_count,)),
+        ],
+        compiler_params=pltpu.CompilerParams(collective_id=collective_id, has_side_effects=True),
+        name="total_gains",
+    )(own)
+
+
+def split_heads_columns(rows_by_columns):
+    rows = rows_by_columns.shape[0]
+    q_width = HEADS * HEAD_DIM
+    kv_width = KV_HEADS * HEAD_DIM
+    query = rows_by_columns[:, :q_width].reshape(rows, KV_HEADS, q_width // KV_HEADS)
+    key = rows_by_columns[:, q_width : q_width + kv_width].reshape(rows, KV_HEADS, HEAD_DIM)
+    value = rows_by_columns[:, q_width + kv_width :].reshape(rows, KV_HEADS, HEAD_DIM)
+    return jnp.concatenate([query, key, value], axis=2).transpose(1, 0, 2)
+
+
+def join_heads_columns(by_head):
+    rows = by_head.shape[1]
+    q_each = HEADS // KV_HEADS * HEAD_DIM
+    ordered = by_head.transpose(1, 0, 2)
+    return jnp.concatenate(
+        [
+            ordered[:, :, :q_each].reshape(rows, -1),
+            ordered[:, :, q_each : q_each + HEAD_DIM].reshape(rows, -1),
+            ordered[:, :, q_each + HEAD_DIM :].reshape(rows, -1),
+        ],
+        axis=1,
+    )
+
+
+def on_device_split(
+    tokens,
+    output_cotangent,
+    sequence_lengths,
+    block_order,
+    attn_input,
+    input_moment,
+    input_square,
+    attn_output,
+    output_moment,
+    output_square,
+    gate_up,
+    gateup_moment,
+    gateup_square,
+    down_weight,
+    down_moment,
+    down_square,
+    norm_gains,
+    gains_moment,
+    gains_square,
+):
+    row_count, model_width = tokens.shape
+    head_groups = HEADS // KV_HEADS
+    q_each = head_groups * HEAD_DIM
+    score_scale = HEAD_DIM ** (-0.5)
+    gain_one = norm_gains[:model_width]
+    gain_two = norm_gains[model_width : 2 * model_width]
+    gain_query = norm_gains[2 * model_width : 2 * model_width + HEAD_DIM]
+    gain_key = norm_gains[2 * model_width + HEAD_DIM :]
+    seq_lens = sequence_lengths[0]
+    order_row = block_order[0]
+    context_count = lax.axis_size("cp")
+    data_count = lax.axis_size("dp")
+    group_rows = context_count * row_count
+    shard_rows = attn_input.shape[0]
+    down_rows = down_weight.shape[0]
+    offsets = jnp.arange(row_count, dtype=jnp.int32)
+    positions = (order_row[:, None] * row_count + offsets[None, :]).reshape(group_rows)
+    doc_index, seq_offset = locate(positions, seq_lens)
+    cosine, sine = rope_tables(seq_offset)
+    x_float = tokens.astype(jnp.float32)
+    hat_one, inv_one = rms_parts(x_float)
+    gateup_send = (
+        gate_up.astype(jnp.bfloat16)
+        .reshape(shard_rows, 2, data_count, context_count, down_rows)
+        .transpose(1, 3, 0, 2, 4)
+        .reshape(2, context_count, shard_rows, data_count * down_rows)
+    )
+    down_part = lax.all_gather(down_weight.astype(jnp.bfloat16), "dp", axis=0, tiled=True)
+    (
+        normed_one,
+        normed_two,
+        cotangent_all,
+        input_part,
+        output_all,
+        gateup_part,
+        raw,
+        flat_parts,
+        log_total,
+        residual,
+    ) = front(
+        tokens,
+        gain_one,
+        gain_two,
+        gain_query,
+        gain_key,
+        cosine.T,
+        sine.T,
+        positions,
+        positions - seq_offset,
+        split_heads_columns(attn_input.astype(jnp.bfloat16)),
+        attn_output.astype(jnp.bfloat16),
+        gateup_send[0],
+        gateup_send[1],
+        output_cotangent,
+        data_count,
+        context_count,
+    )
+    normed_one = normed_one.reshape(group_rows, model_width)
+    normed_two = normed_two.reshape(group_rows, model_width)
+    cotangent_all = cotangent_all.reshape(group_rows, model_width)
+    input_part = input_part.reshape(model_width, -1)
+    output_all = output_all.reshape(HEADS * HEAD_DIM, model_width)
+    gateup_part = gateup_part.reshape(2, model_width, -1)
+    flat_parts = flat_parts.reshape(HEADS * HEAD_DIM, row_count)
+    projected = raw.T
+    query_raw = projected[:, :q_each].reshape(group_rows, head_groups, HEAD_DIM)
+    key_raw = projected[:, q_each : q_each + HEAD_DIM].reshape(group_rows, 1, HEAD_DIM)
+    values = projected[:, q_each + HEAD_DIM :].astype(jnp.bfloat16)
+    hat_query, inv_query = rms_parts(query_raw)
+    hat_key, inv_key = rms_parts(key_raw)
+    queries = rotate(hat_query * gain_query, cosine, sine).astype(jnp.bfloat16)
+    keys = rotate(hat_key * gain_key, cosine, sine).astype(jnp.bfloat16)[:, 0]
+    hat_two, inv_two = rms_parts(residual)
+    gate_part = jnp.dot(normed_two, gateup_part[0], preferred_element_type=jnp.float32)
+    up_part = jnp.dot(normed_two, gateup_part[1], preferred_element_type=jnp.float32)
+    gate_sig = jax.nn.sigmoid(gate_part)
+    gate_act = gate_part * gate_sig
+    hidden = (gate_act * up_part).astype(jnp.bfloat16)
+    d_hidden = contract_cols(cotangent_all, down_part)
+    d_gate = d_hidden * up_part * (gate_sig * (1.0 + gate_part * (1.0 - gate_sig)))
+    d_up = d_hidden * gate_act
+    d_gate = d_gate.astype(jnp.bfloat16)
+    d_up = d_up.astype(jnp.bfloat16)
+    d_normed_two = scatter_line(
+        (contract_cols(d_gate, gateup_part[0]) + contract_cols(d_up, gateup_part[1]))
+        .astype(jnp.bfloat16)
+        .reshape(context_count, row_count, model_width),
+        3,
+        "scatter_second",
+    )
+    grad_gain_two = jnp.sum(d_normed_two * hat_two, axis=0)
+    d_residual = output_cotangent.astype(jnp.float32) + norm_back(
+        d_normed_two * gain_two, hat_two, inv_two
+    )
+    d_branch = d_residual.astype(jnp.bfloat16)
+    d_flat = contract_cols(d_branch, output_all).astype(jnp.bfloat16)
+    d_attended = swap_blocks(
+        d_flat.reshape(row_count, context_count, q_each).transpose(1, 0, 2), 4, "swap_back"
+    ).reshape(group_rows, head_groups, HEAD_DIM)
+    allowed = (doc_index[:, None] == doc_index[None, :]) & (
+        positions[None, :] <= positions[:, None]
+    )
+    scores = (
+        jnp.einsum("qgd,kd->gqk", queries, keys, preferred_element_type=jnp.float32) * score_scale
+    )
+    probs = jnp.exp(jnp.where(allowed, scores, masked_score) - log_total[:, :, None])
+    probs_bf = probs.astype(jnp.bfloat16)
+    d_probs = jnp.einsum("qgd,kd->gqk", d_attended, values, preferred_element_type=jnp.float32)
+    delta = jnp.sum(probs * d_probs, axis=-1, keepdims=True)
+    d_scores = (probs * (d_probs - delta)).astype(jnp.bfloat16)
+    d_query_sum = (
+        jnp.einsum("gqk,kd->qgd", d_scores, keys, preferred_element_type=jnp.float32) * score_scale
+    )
+    d_key_sum = (
+        jnp.einsum("gqk,qgd->kd", d_scores, queries, preferred_element_type=jnp.float32)
+        * score_scale
+    )
+    d_value = jnp.einsum("gqk,qgd->kd", probs_bf, d_attended, preferred_element_type=jnp.float32)
+    d_query_rot = rotate(d_query_sum, cosine, -sine)
+    grad_gain_query = jnp.sum(d_query_rot * hat_query, axis=(0, 1))
+    d_query_raw = norm_back(d_query_rot * gain_query, hat_query, inv_query)
+    d_key_rot = rotate(d_key_sum[:, None, :], cosine, -sine)
+    grad_gain_key = jnp.sum(d_key_rot * hat_key, axis=(0, 1))
+    d_key_raw = norm_back(d_key_rot * gain_key, hat_key, inv_key)
+    d_projected = jnp.concatenate(
+        [
+            d_query_raw.reshape(group_rows, q_each),
+            d_key_raw.reshape(group_rows, HEAD_DIM),
+            d_value,
+        ],
+        axis=1,
+    ).astype(jnp.bfloat16)
+    d_normed_one = scatter_line(
+        contract_cols(d_projected, input_part)
+        .astype(jnp.bfloat16)
+        .reshape(context_count, row_count, model_width),
+        5,
+        "scatter_first",
+    )
+    grad_gain_one = jnp.sum(d_normed_one * hat_one, axis=0)
+    token_gradient = d_residual + norm_back(d_normed_one * gain_one, hat_one, inv_one)
+    mixed = (
+        residual
+        + scatter_line(
+            jnp.dot(hidden, down_part, preferred_element_type=jnp.float32)
+            .astype(jnp.bfloat16)
+            .reshape(context_count, row_count, model_width),
+            6,
+            "scatter_down",
+        )
+    ).astype(jnp.bfloat16)
+
+    def owned_rows(grad, collective_id, name):
+        share = lax.psum_scatter(
+            grad.astype(jnp.bfloat16), "dp", scatter_dimension=0, tiled=True
+        )
+        return swap_blocks(share.reshape(context_count, shard_rows, -1), collective_id, name)
+
+    grad_down = lax.psum_scatter(
+        contract_rows(hidden, cotangent_all).astype(jnp.bfloat16),
+        "dp",
+        scatter_dimension=0,
+        tiled=True,
+    ).astype(jnp.float32)
+    grad_gateup = [
+        owned_rows(contract_rows(normed_two, part), 7 + index, "swap_gateup")
+        .reshape(context_count, shard_rows, data_count, down_rows)
+        .transpose(1, 2, 0, 3)
+        .reshape(shard_rows, -1)
+        for index, part in enumerate((d_gate, d_up))
+    ]
+    grad_gateup = jnp.concatenate(grad_gateup, axis=1).astype(jnp.float32)
+    grad_output = lax.psum_scatter(
+        lax.psum_scatter(
+            jnp.dot(flat_parts, d_branch, preferred_element_type=jnp.float32).astype(jnp.bfloat16),
+            "dp",
+            scatter_dimension=0,
+            tiled=True,
+        ),
+        "cp",
+        scatter_dimension=0,
+        tiled=True,
+    ).astype(jnp.float32)
+    grad_input = join_heads_columns(
+        owned_rows(contract_rows(normed_one, d_projected), 9, "swap_input")
+    ).astype(jnp.float32)
+    gain_grads = jnp.concatenate([grad_gain_one, grad_gain_two, grad_gain_query, grad_gain_key])
+    gain_grads = total_everywhere(
+        gain_grads.reshape(-1, 128), data_count, context_count, 10
+    ).reshape(-1)
+    input_next, input_moment_next, input_square_next = adam_update(
+        attn_input, input_moment, input_square, grad_input, rate_input, weight_decay
+    )
+    output_next, output_moment_next, output_square_next = adam_update(
+        attn_output, output_moment, output_square, grad_output, rate_output, weight_decay
+    )
+    gateup_next, gateup_moment_next, gateup_square_next = adam_update(
+        gate_up, gateup_moment, gateup_square, grad_gateup, rate_gateup, weight_decay
+    )
+    down_next, down_moment_next, down_square_next = adam_update(
+        down_weight, down_moment, down_square, grad_down, rate_down, weight_decay
+    )
+    gains_next, gains_moment_next, gains_square_next = adam_update(
+        norm_gains, gains_moment, gains_square, gain_grads, rate_gains, 0.0
+    )
+    return (
+        mixed,
+        token_gradient,
+        input_next,
+        input_moment_next,
+        input_square_next,
+        output_next,
+        output_moment_next,
+        output_square_next,
+        gateup_next,
+        gateup_moment_next,
+        gateup_square_next,
+        down_next,
+        down_moment_next,
+        down_square_next,
+        gains_next,
+        gains_moment_next,
+        gains_square_next,
+    )
+
+
 def solution(mesh):
     in_specs = (
         P(("dp", "cp"), None),
@@ -448,6 +1478,8 @@
         P(),
         P(),
     )
+    sizes = (mesh.shape["dp"], mesh.shape["cp"])
+    body = on_device_split if sizes == (4, KV_HEADS) else on_device
     return jax.shard_map(
-        on_device, mesh=mesh, in_specs=in_specs, out_specs=out_specs, check_vma=False
-    )
+        body, mesh=mesh, in_specs=in_specs, out_specs=out_specs, check_vma=False
+    )

time: 1570 us -> 649 us (0.41)
  waiting for transfers between devices: 1210 us -> 81.8 us
  Pallas kernels: 0 us -> 351 us
  matrix products: 157 us -> 101 us
  other arithmetic: 96.5 us -> 42.2 us
  blocking collectives: 38 us -> 0 us
    reduce_scatter x4 -> x5, waiting for transfers between devices: 724 us -> 81.7 us  [the longest x1 52.2 us: on_device_split(): lax.psum_scatter(jnp.dot(flat_parts, d_branch, preferred_element_type=jnp...]
    all_gather x5 -> x1, waiting for transfers between devices: 481 us -> 0.01 us  [on_device_split(): lax.all_gather(down_weight.astype(jnp.bfloat16), 'dp', axis=0, tiled=True)]
    pallas_call x0 -> x9, Pallas kernels: none -> 351 us  [the longest x1 148 us: front(): pl.pallas_call(functools.partial(front_kernel, 2 * rows), out_shape=[jax....]
    concatenate x2 -> x0, other arithmetic: 38.6 us -> none  [the longest x1 36.9 us: wide_terms(): jnp.concatenate([contract_rows(first_src, d_projected), contract_rows(att...]
    psum x1 -> x0, blocking collectives: 38 us -> none  [on_device(): lax.psum(jnp.concatenate([grad_gain_one, grad_gain_two, grad_gain_query,...]
    dot_general x18 -> x9, matrix products: 74.9 us -> 45.1 us  [the longest x1 10.3 us: on_device_split(): jnp.einsum('qgd,kd->gqk', d_attended, values, preferred_element_type=jnp....]
    reshape x3 -> x21, local copies, waits for them, and re-layouts: 1.83 us -> 22 us  [the longest x4 8.89 us: on_device_split(): grad_gateup = [owned_rows(contract_rows(normed_two, part), 7 + index, 'sw...]
    dot_general x4, matrix products: 38.3 us -> 21.7 us  [contract_rows(): lax.dot_general(left, right, (((0,), (0,)), ((), ())), preferred_element_...]
  transfers between devices with their start and end apart: 10 -> 7, of which waited for: 8 -> 2; matrix products, arithmetic and copies ran while one was open for 13% -> 17% of each run, Pallas kernels for 0% -> 39%
where the time goes in v1:
time: 649 us; the launch traced here: 645 us
  Pallas kernels  351 us (54%)
  matrix products  101 us (16%)
  waiting for transfers between devices  81.8 us (13%)
  local copies, waits for them, and re-layouts  53.6 us (8%)
  other arithmetic  42.2 us (7%)
  between operations  15.6 us (2%)
    pallas_call x1, Pallas kernels, front(): pl.pallas_call(functools.partial(front_kernel, 2 * rows), out_shape=[jax....  148 us
    pallas_call x3, Pallas kernels, scatter_line(): pl.pallas_call(functools.partial(scatter_kernel, depth), out_shape=jax.Sh...  126 us
    pallas_call x4, Pallas kernels, swap_blocks(): pl.pallas_call(functools.partial(swap_kernel, source.shape[0]), out_shape...  64.7 us
    reduce_scatter x1, waiting for transfers between devices, on_device_split(): lax.psum_scatter(jnp.dot(flat_parts, d_branch, preferred_element_type=jnp...  52.2 us
    dot_general x5, matrix products, contract_cols(): lax.dot_general(left, right, (((1,), (1,)), ((), ())), preferred_element_...  34.2 us
    reduce_scatter x1, waiting for transfers between devices, on_device_split(): lax.psum_scatter(lax.psum_scatter(jnp.dot(flat_parts, d_branch, preferred...  29.4 us
    dot_general x4, matrix products, contract_rows(): lax.dot_general(left, right, (((0,), (0,)), ((), ())), preferred_element_...  21.7 us
    unnamed x143, local copies, waits for them, and re-layouts  15.8 us
  transfers between devices with their start and end apart: 7, of which 2 were waited for; matrix products, arithmetic and copies ran while one was open for 17% of the time, Pallas kernels for 39%

profile of v1, /device:TPU:0, one launch (start us, length us, event | category | flops | bytes accessed | tf_op | source)
XLA Modules:
  0.0 645.5 jit_solution(5666145357623187652)
XLA Ops:
  18.6 5.9 reshape.484
  30.9 148.2 %front.1 = (bf16[8,128,1536]{2,1,0:T(8,128)(2,1)}, bf16[8,128,1536]{2,1,0:T(8,128)(2,1)}, bf16[8,128,1536]{2,1,0:T(8,128)(2,1)}, bf16[4,8,48,320]{3,2,1,0:T(8,12...) custom-call(bf16[128,1536]{1,0:T(8,128)(2,1)} %tokens_ref.1, ...), custom_call_target="tpu_custom_call" | custom-call | tf_op jit(solution)/shard_map/front/pallas_call | solution.py:879
  187.8 6.3 fusion.38
  201.9 4.9 fusion.92
  206.9 10.2 %multiply_convert_fusion = (bf16[1024,864]{0,1:T(8,128)(2,1)S(1)}, bf16[1024,864]{0,1:T(8,128)(2,1)S(1)}, bf16[1024,864]{0,1:T(8,128)(2,1)}) fusion(f32[1024,864]{0,1:T(8,128)} %fusion.91, f32[1024,864]{0,1:T(8,128)} %fusion.92, bf16[1024,1536]{1,0:T(8,128)(2,1)} %bitcast.206, bf16[864,1536]{1,0:T(8,128)(2,1)} %all-gather.2.cloned.1.call-done), kind=kOutput, calls=%fused_computation.17 | convolution fusion | flops 2731180032 | bytes 18186240 | tf_op jit(solution)/shard_map/dot_general | solution.py:84
  217.0 15.4 %fusion.93 = f32[1024,1536]{1,0:T(8,128)S(1)} fusion(bf16[1024,864]{0,1:T(8,128)(2,1)S(1)} %get-tuple-element.59, bf16[1536,864]{1,0:T(8,128)(2,1)S(1)} %bitcast.192), kind=kOutput, calls=%fused_computation.169 | convolution fusion | flops 2717908992 | bytes 10715136 | tf_op jit(solution)/shard_map/dot_general | solution.py:84
  236.4 41.1 %scatter_second.1 = f32[128,1536]{1,0:T(8,128)S(1)} custom-call(bf16[8,128,1536]{2,1,0:T(8,128)(2,1)S(1)} %bitcast.166), custom_call_target="tpu_custom_call" | custom-call | tf_op jit(solution)/shard_map/scatter_second/pallas_call | solution.py:1103
  282.1 42.5 %scatter_down.1 = f32[128,1536]{1,0:T(8,128)S(1)} custom-call(bf16[8,128,1536]{2,1,0:T(8,128)(2,1)S(1)} %bitcast.167), custom_call_target="tpu_custom_call" | custom-call | tf_op jit(solution)/shard_map/scatter_down/pallas_call | solution.py:1103
  330.2 15.6 %swap_back.1 = bf16[8,128,192]{2,1,0:T(8,128)(2,1)} custom-call(bf16[8,128,192]{2,1,0:T(8,128)(2,1)} %bitcast.193), custom_call_target="tpu_custom_call" | custom-call | tf_op jit(solution)/shard_map/swap_back/pallas_call | solution.py:938
  348.1 8.1 %fusion.20 = bf16[1024,64]{0,1:T(8,128)(2,1)S(1)} fusion(bf16[1024,3,64]{0,2,1:T(8,128)(2,1)} %reshape.492, f32[1024,1024,3]{1,0,2:T(8,128)} %fusion.38, f32[3,1024]{1,0:T(4,128)} %get-tuple-element.32, pred[1024,1024]{0,1:T(8,128)(4,1)S(1)} %compare_and_fusion), kind=kOutput, calls=%fused_computation.46 | convolution fusion | flops 415301632 | bytes 14168064 | tf_op jit(solution)/shard_map/gqk,qgd->kd/dot_general | solution.py:1331
  356.3 10.3 %fusion = (f32[3,1024]{1,0:T(4,128)S(1)}, f32[1024,1024,3]{1,0,2:T(8,128)}) fusion(f32[1024,1024,3]{1,0,2:T(8,128)} %fusion.38, f32[3,1024]{1,0:T(4,128)S(1)} %copy-done.33, pred[1024,1024]{0,1:T(8,128)(4,1)S(1)} %compare_and_fusion, bf16[1024,3,64]{0,2,1:T(8,128)(2,1)S(1)} %copy-done.13, f32[1024,320]{0,1:T(8,128)S(1)} %bitcast.177), kind=kOutput, calls=%fused_computation.2 | convolution fusion | flops 418378752 | bytes 26767360 | tf_op jit(solution)/shard_map/qgd,kd->gqk/dot_general | solution.py:1321
  366.6 6.9 %fusion.2 = bf16[3,1024,1024]{1,2,0:T(8,128)(2,1)S(1)} fusion(f32[1024,1024,3]{1,0,2:T(8,128)} %get-tuple-element.97, f32[1024,1024,3]{1,0,2:T(8,128)S(1)} %bitcast.169, f32[3,1024]{1,0:T(4,128)S(1)} %get-tuple-element.96, f32[3,1024]{1,0:T(4,128)S(1)} %copy-done.33, pred[1024,1024]{0,1:T(8,128)(4,1)S(1)} %compare_and_fusion), kind=kLoop, calls=%fused_computation.4 | loop fusion | flops 18874368 | bytes 32530432 | tf_op jit(solution)/shard_map/convert_element_type | solution.py:1323
  382.7 6.8 %convolution_convert_fusion.3 = bf16[1536,864]{0,1:T(8,128)(2,1)} fusion(bf16[1024,864]{0,1:T(8,128)(2,1)} %copy-done.61, bf16[1024,1536]{1,0:T(8,128)(2,1)} %bitcast.208), kind=kOutput, calls=%fused_computation.22 | convolution fusion | flops 2719236096 | bytes 7569408 | tf_op jit(solution)/shard_map/dot_general | solution.py:78
  394.1 6.8 %convolution_convert_fusion.4 = bf16[1536,864]{0,1:T(8,128)(2,1)} fusion(bf16[1024,864]{0,1:T(8,128)(2,1)} %copy-done.58, bf16[1024,1536]{1,0:T(8,128)(2,1)} %bitcast.209), kind=kOutput, calls=%fused_computation.23 | convolution fusion | flops 2719236096 | bytes 7569408 | tf_op jit(solution)/shard_map/dot_general | solution.py:78
  405.7 6.8 %convolution_convert_fusion.5 = bf16[864,1536]{1,0:T(8,128)(2,1)} fusion(bf16[1024,864]{0,1:T(8,128)(2,1)} %get-tuple-element.60, bf16[1024,1536]{1,0:T(8,128)(2,1)} %bitcast.207), kind=kOutput, calls=%fused_computation.24 | convolution fusion | flops 2719236096 | bytes 7569408 | tf_op jit(solution)/shard_map/dot_general | solution.py:78
  421.5 42.7 %scatter_first.1 = f32[128,1536]{1,0:T(8,128)S(1)} custom-call(bf16[8,128,1536]{2,1,0:T(8,128)(2,1)S(1)} %bitcast.165), custom_call_target="tpu_custom_call" | custom-call | tf_op jit(solution)/shard_map/scatter_first/pallas_call | solution.py:1103
  465.6 11.8 %total_gains.1 = f32[25,128]{1,0:T(8,128)} custom-call(f32[25,128]{1,0:T(8,128)} %bitcast.201), custom_call_target="tpu_custom_call" | custom-call | tf_op jit(solution)/shard_map/total_gains/pallas_call | solution.py:1151
  479.9 10.7 %swap_input.1 = bf16[8,48,320]{2,1,0:T(8,128)(2,1)} custom-call(bf16[8,48,320]{2,1,0:T(8,128)(2,1)} %bitcast.200), custom_call_target="tpu_custom_call" | custom-call | tf_op jit(solution)/shard_map/swap_input/pallas_call | solution.py:938
  494.6 19.2 %swap_gateup.3 = bf16[8,48,864]{2,1,0:T(8,128)(2,1)} custom-call(bf16[8,48,864]{2,1,0:T(8,128)(2,1)} %bitcast.198), custom_call_target="tpu_custom_call" | custom-call | tf_op jit(solution)/shard_map/swap_gateup/pallas_call | solution.py:938
  518.8 19.2 %swap_gateup.2 = bf16[8,48,864]{2,1,0:T(8,128)(2,1)} custom-call(bf16[8,48,864]{2,1,0:T(8,128)(2,1)} %bitcast.199), custom_call_target="tpu_custom_call" | custom-call | tf_op jit(solution)/shard_map/swap_gateup/pallas_call | solution.py:938
  543.6 5.1 multiply_subtract_fusion.1
  548.8 52.2 %reduce-scatter.15.cloned.1.call-done = bf16[384,1536]{1,0:T(8,128)(2,1)} async-done(((bf16[1536,1536]{1,0:T(8,128)(2,1)}), bf16[384,1536]{1,0:T(8,128)(2,1)}) %reduce-scatter.15.cloned.1.call-update) | async-done | bytes 1179664 | tf_op jit(solution)/shard_map/reduce_scatter | solution.py:1387
  601.0 5.7 multiply_subtract_fusion
  606.7 29.4 %reduce-scatter.17.cloned.1.call-done = bf16[48,1536]{1,0:T(8,128)(2,1)} async-done(((bf16[384,1536]{1,0:T(8,128)(2,1)}), bf16[48,1536]{1,0:T(8,128)(2,1)}) %reduce-scatter.17.cloned.1.call-update) | async-done | bytes 147472 | tf_op jit(solution)/shard_map/reduce_scatter | solution.py:1386
  (264 shorter events, 97.8 us)
Async XLA Ops:
  7.2 199.6 %all-gather.2.cloned.1.call-start = ((), (), s32[]{:S(2)}) async-start(), calls=%async_computation.6 | async-start | bytes 3317760 | tf_op jit(solution)/shard_map/all_gather | solution.py:1241
  9.7 470.2 %reduce-scatter.19.cloned.1.call-start = ((), (), s32[]{:S(2)}) async-start(), calls=%async_computation.9 | async-start | bytes 1474560 | tf_op jit(solution)/shard_map/reduce_scatter | solution.py:1367
  30.9 151.9 %copy-start.50 = (f32[64]{0:T(128)S(1)}, f32[64]{0:T(128)}, u32[]{:S(2)}) copy-start(f32[64]{0:T(128)} %get-tuple-element.86) | copy-start | bytes 772
  30.9 152.5 %copy-start.48 = (f32[64]{0:T(128)S(1)}, f32[64]{0:T(128)}, u32[]{:S(2)}) copy-start(f32[64]{0:T(128)} %get-tuple-element.83) | copy-start | bytes 772
  232.5 45.8 %copy-start.55 = (bf16[864,1536]{1,0:T(8,128)(2,1)S(1)}, bf16[864,1536]{1,0:T(8,128)(2,1)}, u32[]{:S(2)}) copy-start(bf16[864,1536]{1,0:T(8,128)(2,1)} %all-gather.2.cloned.1.call-done) | copy-start | bytes 7962628
  232.5 45.8 %copy-start.62 = (bf16[1024,864]{0,1:T(8,128)(2,1)S(1)}, bf16[1024,864]{0,1:T(8,128)(2,1)}, u32[]{:S(2)}) copy-start(bf16[1024,864]{0,1:T(8,128)(2,1)} %get-tuple-element.60) | copy-start | bytes 5308420
  236.3 41.1 %copy-start.2 = (f32[128,1536]{1,0:T(8,128)S(1)}, f32[128,1536]{1,0:T(8,128)}, u32[]{:S(2)}) copy-start(f32[128,1536]{1,0:T(8,128)} %get-tuple-element.27) | copy-start | bytes 2359300
  236.4 41.1 %copy-start.26 = (f32[1536]{0:T(1024)S(1)}, f32[1536]{0:T(1024)}, u32[]{:S(2)}) copy-start(f32[1536]{0:T(1024)} %copy-done.25) | copy-start | bytes 18436
  236.4 89.2 %slice-start.5 = ((s8[4718592]{0:T(1024)(128)(4,1)}), s8[4194304]{0:T(1024)(128)(4,1)S(1)}, s32[]{:S(2)}) async-start(s8[4718592]{0:T(1024)(128)(4,1)} %bitcast.184), calls=%async_computation.18 | async-start | bytes 8388608
  278.3 47.3 %slice-start.6 = ((s8[4718592]{0:T(1024)(128)(4,1)}), s8[524288]{0:T(1024)(128)(4,1)S(1)}, s32[]{:S(2)}) async-start(s8[4718592]{0:T(1024)(128)(4,1)} %bitcast.184), calls=%async_computation.19 | async-start | bytes 1048576
  282.1 42.5 %copy-start.12 = (bf16[128,1536]{1,0:T(8,128)(2,1)S(1)}, bf16[128,1536]{1,0:T(8,128)(2,1)}, u32[]{:S(2)}) copy-start(bf16[128,1536]{1,0:T(8,128)(2,1)} %cotangent_own.1) | copy-start | bytes 1179652
  356.3 23.1 %copy-start.59 = (bf16[1024,64]{0,1:T(8,128)(2,1)}, bf16[1024,64]{0,1:T(8,128)(2,1)S(1)}, u32[]{:S(2)}) copy-start(bf16[1024,64]{0,1:T(8,128)(2,1)S(1)} %fusion.20) | copy-start | bytes 393220
  382.7 112.0 %reduce-scatter.23.cloned.1.call-start = ((), (), s32[]{:S(2)}) async-start(), calls=%async_computation.11 | async-start | bytes 3440640 | tf_op jit(solution)/shard_map/reduce_scatter | solution.py:1367
  394.1 124.7 %reduce-scatter.21.cloned.1.call-start = ((), (), s32[]{:S(2)}) async-start(), calls=%async_computation.10 | async-start | bytes 3440640 | tf_op jit(solution)/shard_map/reduce_scatter | solution.py:1367
  405.7 138.0 %reduce-scatter.25.cloned.1.call-start = ((), (), s32[]{:S(2)}) async-start(), calls=%async_computation.12 | async-start | bytes 3317760
  412.6 188.4 %reduce-scatter.15.cloned.1.call-start = ((), (), s32[]{:S(2)}) async-start(), calls=%async_computation.7 | async-start | bytes 5898240 | tf_op jit(solution)/shard_map/reduce_scatter | solution.py:1387
  417.1 219.0 %reduce-scatter.17.cloned.1.call-start = ((), (), s32[]{:S(2)}) async-start(), calls=%async_computation.8 | async-start | bytes 1327104 | tf_op jit(solution)/shard_map/reduce_scatter | solution.py:1386
  421.5 42.8 %copy-start.5 = (f32[1024,192]{0,1:T(8,128)S(1)}, f32[1024,192]{0,1:T(8,128)}, u32[]{:S(2)}) copy-start(f32[1024,192]{0,1:T(8,128)} %get-tuple-element.65) | copy-start | bytes 2359300
  421.5 43.1 %copy-start.24 = (f32[1536]{0:T(1024)S(1)}, f32[1536]{0:T(1024)}, u32[]{:S(2)}) copy-start(f32[1536]{0:T(1024)} %copy-done.23) | copy-start | bytes 18436
  421.5 43.4 %copy-start.42 = (f32[1536]{0:T(1024)S(1)}, f32[1536]{0:T(1024)}, u32[]{:S(2)}) copy-start(f32[1536]{0:T(1024)} %get-tuple-element.39) | copy-start | bytes 18436
  421.5 55.9 %copy-start.32 = (f32[3200]{0:T(1024)S(1)}, f32[3200]{0:T(1024)}, u32[]{:S(2)}) copy-start(f32[3200]{0:T(1024)} %param.35) | copy-start | bytes 38404
  421.5 55.9 %copy-start.43 = (f32[3200]{0:T(1024)S(1)}, f32[3200]{0:T(1024)}, u32[]{:S(2)}) copy-start(f32[3200]{0:T(1024)} %param.36) | copy-start | bytes 38404
  421.5 55.9 %copy-start.44 = (f32[3200]{0:T(1024)S(1)}, f32[3200]{0:T(1024)}, u32[]{:S(2)}) copy-start(f32[3200]{0:T(1024)} %param.37) | copy-start | bytes 38404
  543.6 57.4 %copy-start.1 = (f32[48,13824]{1,0:T(8,128)S(1)}, f32[48,13824]{1,0:T(8,128)}, u32[]{:S(2)}) copy-start(f32[48,13824]{1,0:T(8,128)} %param.29) | copy-start | bytes 7962628
  (53 other events, 356.1 us)
Sparse Core Ops, SparseCore 0:
  10.5 42.6 all-gather.1
  382.8 27.0 reduce-scatter.18
  412.9 40.6 reduce-scatter.22
  456.5 41.2 reduce-scatter.20
  501.1 39.8 reduce-scatter.24
  543.8 57.0 reduce-scatter.14
  603.3 32.8 reduce-scatter.16
